TPU v7x, 32 devices: a whole 2x2x4 slice. The times are simulated.
32 devices in a mesh: dp: 4 (over y, x), expert: 8 (over z, core).
Axes of the slice: x: 2, y: 2, z: 4, core: 2. Of those that a mesh axis runs over, the one named last changes fastest.
Arguments:
- unit_codes: bfloat16 [16, 256, 1536], P('expert', 'dp'), may hold values from -4 to 4
- block_scales: float32 [16, 12, 256], P('expert', None, 'dp'), may hold values from 0.05 to 2
- pair_list: int32 [32, 2], replicated, may hold values from 0 to 15, as said below
Outputs:
- left_best: float32 [8, 4, 1536], P('expert', None, 'dp')
- right_best: float32 [8, 4, 1536], P('expert', None, 'dp')
Inputs may be any that keep to these rules, and one draw needn't show every extreme that they name: `pair_list`: row 4 * e + s names as its first expert one of 2 * e to 2 * e + 1, and as its second one of the 2 experts starting at 2 * ((e + o_s) mod n), with n = 8; the offsets o_s are nonzero, distinct over s, include 1, n / 2 and n - 1, and are the same for every e.
All inputs are finite; a program needn't handle non-finite values.
Results may differ from a plain program's by a relative error of at most 0.0017.
Values may be sent and summed in bfloat16 or wider, within the bound.
A program may use at most 128 MiB of HBM per device.

v0:
```python
import math

import jax
import jax.numpy as jnp
from jax import lax
from jax.sharding import PartitionSpec as P

EPSILON = 1e-06


def body(unit_codes, block_scales, pair_list):
    num_devices = lax.axis_size("expert")
    groups = lax.axis_size("dp")
    my_index = lax.axis_index("expert")
    dp_index = lax.axis_index("dp")
    per_device, row_count, unit_count = unit_codes.shape
    num_blocks = block_scales.shape[1]
    block_len = unit_count // num_blocks
    slice_width = unit_count // groups
    factor = jnp.transpose(block_scales, (0, 2, 1))[:, :, :, None]
    acts = (
        unit_codes.astype(jnp.float32).reshape(per_device, row_count, num_blocks, block_len)
        * factor
    )
    acts = acts.reshape(per_device, row_count, unit_count).astype(jnp.bfloat16)
    slot_count = pair_list.shape[0] // num_devices
    pair_table = pair_list.reshape(num_devices, slot_count, 2)
    my_pairs = lax.dynamic_index_in_dim(pair_table, my_index, 0, keepdims=False)
    left_local = my_pairs[:, 0] % per_device
    right_dev = my_pairs[:, 1] // per_device
    is_asked = pair_table[:, :, 1] // per_device == my_index
    chosen = jnp.sum(jnp.where(is_asked, pair_table[:, :, 1] % per_device, 0), axis=1)
    in_use = jnp.any(is_asked, axis=1)
    chooser = ((chosen[:, None] == jnp.arange(per_device)[None, :]) & in_use[:, None]).astype(
        jnp.bfloat16
    )
    own_full = lax.all_gather(acts, "dp", axis=1, tiled=True)
    flattened = acts.reshape(per_device, -1)
    outbound = jnp.dot(chooser, flattened, preferred_element_type=jnp.float32).astype(jnp.bfloat16)
    received = lax.all_to_all(
        outbound.reshape((num_devices,) + acts.shape[1:]),
        "expert",
        split_axis=0,
        concat_axis=0,
        tiled=True,
    )
    wanted = jnp.take(received, right_dev, axis=0)
    partner = lax.all_to_all(wanted, "dp", split_axis=2, concat_axis=1, tiled=True)
    all_rows = partner.shape[1]
    own_square = (
        jnp.einsum("era,era->ea", own_full, own_full, preferred_element_type=jnp.float32) / all_rows
    )
    inv_own = 1.0 / jnp.sqrt(own_square + EPSILON)
    part_square = (
        jnp.einsum("srb,srb->sb", partner, partner, preferred_element_type=jnp.float32) / all_rows
    )
    inv_part = 1.0 / jnp.sqrt(part_square + EPSILON)

    def single(member):
        expert_pick, partner_block, inv_unit = member
        left_rows = jnp.take(own_full, expert_pick, axis=0)
        gram_block = jnp.einsum(
            "ra,rb->ab", left_rows, partner_block, preferred_element_type=jnp.float32
        )
        correlation = (
            gram_block
            / all_rows
            * jnp.take(inv_own, expert_pick, axis=0)[:, None]
            * inv_unit[None, :]
        )
        return (jnp.max(correlation, axis=1), jnp.max(correlation, axis=0))

    def several(member):
        return jax.vmap(single)(member)

    bundle = math.gcd(slot_count, 4)
    stacked = (
        left_local.reshape(-1, bundle),
        partner.reshape(-1, bundle, all_rows, slice_width),
        inv_part.reshape(-1, bundle, slice_width),
    )
    left_part, right_part = lax.map(several, stacked)
    left_part = left_part.reshape(slot_count, unit_count)
    right_part = right_part.reshape(slot_count, slice_width)
    left_all = lax.pmax(left_part, "dp")
    left_out = lax.dynamic_slice_in_dim(left_all, dp_index * slice_width, slice_width, 1)
    target = (right_dev[:, None] == jnp.arange(num_devices)[None, :]).astype(jnp.float32)
    outgoing = jnp.dot(
        target.T, right_part, precision=lax.Precision.HIGHEST, preferred_element_type=jnp.float32
    )
    returned = lax.all_to_all(outgoing, "expert", split_axis=0, concat_axis=0, tiled=True)
    offsets = pair_table[0, :, 1] // per_device
    source_dev = (my_index - offsets) % num_devices
    right_out = jnp.take(returned, source_dev, axis=0)
    return (left_out[None], right_out[None])


def solution(mesh):
    in_specs = (P("expert", "dp", None), P("expert", None, "dp"), P())
    out_specs = (P("expert", None, "dp"), P("expert", None, "dp"))
    return jax.shard_map(body, mesh=mesh, in_specs=in_specs, out_specs=out_specs, check_vma=False)
```

profile of v0, /device:TPU:0, one launch (start us, length us, event | category | flops | bytes accessed | tf_op | source)
XLA Modules:
  0.0 113.2 jit_solution(17694646729727842664)
XLA Ops:
  7.2 0.8 reshape.207
  8.0 0.1 copy.15
  8.1 0.8 copy.14
  8.9 0.3 mul.42
  9.3 0.1 mul.43
  9.5 0.4 copy.38
  9.9 0.6 convolution_convert_fusion
  10.5 1.6 %copy.16 = bf16[8,64,1536]{2,1,0:T(8,128)(2,1)} copy(bf16[8,64,1536]{2,0,1:T(8,128)(2,1)S(1)} %bitcast.89) | data formatting | bytes 3145728 | tf_op jit(solution)/shard_map/reshape | solution.py:41
  12.1 6.3 %all-to-all-start = ((bf16[8,64,1536]{2,1,0:T(8,128)(2,1)}), bf16[8,64,1536]{2,1,0:T(8,128)(2,1)S(1)}, u32[]{:S(2)}, u32[]{:S(2)}) async-start(bf16[8,64,1536]{2,1,0:T(8,128)(2,1)} %copy.16), calls=%async_computation | async-start | bytes 3145728 | tf_op jit(solution)/shard_map/all_to_all | solution.py:40
  18.5 0.7 all-gather.2.cloned.1.call-update
  19.3 34.3 %all-gather.2.cloned.1.call-done = bf16[2,256,1536]{2,1,0:T(8,128)(2,1)} async-done(((bf16[2,64,1536]{2,1,0:T(8,128)(2,1)}), bf16[2,256,1536]{2,1,0:T(8,128)(2,1)}) %all-gather.2.cloned.1.call-update) | async-done | bytes 1572880 | tf_op jit(solution)/shard_map/all_gather | solution.py:37
  53.6 1.7 %fusion.2 = f32[2,1536]{1,0:T(2,128)S(1)} fusion(bf16[2,256,1536]{2,1,0:T(8,128)(2,1)} %all-gather.2.cloned.1.call-done), kind=kLoop, calls=%fused_computation.9 | loop fusion | flops 2356224 | bytes 1585152 | tf_op jit(solution)/shard_map/era,era->ea/dot_general | solution.py:51
  55.4 0.9 all-to-all-done
  56.3 0.6 gather_fusion.1
  56.9 1.0 broadcast_select_fusion
  57.9 2.7 %copy.17 = bf16[4,64,1536]{1,0,2:T(4,128)(2,1)S(1)} copy(bf16[4,64,1536]{2,1,0:T(8,128)(2,1)} %broadcast_select_fusion) | data formatting | bytes 1572864 | tf_op jit(solution)/shard_map/jit(_take)/select_n | solution.py:47
  60.6 2.4 %reshape.246 = bf16[4,2,49152]{2,1,0:T(2,128)(2,1)} reshape(bf16[1536,4,64]{2,1,0:T(4,128)(2,1)S(1)} %bitcast.90) | data formatting | bytes 1572864
  63.0 3.7 %all-to-all-start.1 = ((bf16[4,2,49152]{2,1,0:T(2,128)(2,1)}), bf16[4,2,49152]{2,1,0:T(2,128)(2,1)S(1)}, u32[]{:S(2)}, u32[]{:S(2)}) async-start(bf16[4,2,49152]{2,1,0:T(2,128)(2,1)} %reshape.246), calls=%async_computation.1 | async-start | bytes 1572864 | tf_op jit(solution)/shard_map/all_to_all | solution.py:48
  66.7 0.6 gather_fusion.2
  67.3 2.4 %gather_fusion = bf16[4,256,1536]{2,1,0:T(8,128)(2,1)} fusion(bf16[2,256,1536]{2,1,0:T(8,128)(2,1)S(1)} %copy-done, s32[1024]{0:T(1024)S(1)} %pad_clamp_fusion.2), kind=kCustom, calls=%fused_computation | custom fusion | bytes 6291472 | tf_op jit(solution)/shard_map/while/body/eval_jaxpr/vmap(jit(_take))/gather | solution.py:61
  69.8 7.6 %all-to-all-done.1 = bf16[4,2,49152]{2,1,0:T(2,128)(2,1)S(1)} async-done(((bf16[4,2,49152]{2,1,0:T(2,128)(2,1)}), bf16[4,2,49152]{2,1,0:T(2,128)(2,1)S(1)}, u32[]{:S(2)}, u32[]{:S(2)}) %all-to-all-start.1) | async-done | bytes 786464 | tf_op jit(solution)/shard_map/all_to_all | solution.py:48
  77.4 1.2 %reshape.247 = bf16[1536,4,64]{2,1,0:T(4,128)(2,1)S(1)} reshape(bf16[4,2,49152]{2,1,0:T(2,128)(2,1)S(1)} %all-to-all-done.1) | data formatting | bytes 1572864
  78.6 1.0 copy.18
  79.6 0.3 fusion.6
  79.9 4.6 %fusion = (f32[4,384]{1,0:T(4,128)S(1)}, f32[4,1536]{1,0:T(4,128)S(1)}) fusion(f32[4,384]{1,0:T(4,128)S(1)} %add_rsqrt_fusion.1, f32[4,1536]{1,0:T(4,128)S(1)} %select_multiply_fusion, bf16[4,256,384]{2,1,0:T(8,128)(2,1)S(1)} %bitcast.93, bf16[4,256,1536]{2,1,0:T(8,128)(2,1)} %gather_fusion, pred[4]{0:T(512)(128)(4,1)S(1)} %get-tuple-element.20), kind=kOutput, calls=%fused_computation.6 | convolution fusion | flops 1218961920 | bytes 3993604 | tf_op jit(solution)/shard_map/while/body/eval_jaxpr/vmap(ra,rb->ab)/dot_general | solution.py:62
  84.5 0.3 convolution_bitcast_fusion
  84.8 0.6 copy.20
  85.4 3.9 %all-to-all-start.2 = ((f32[8,1,384]{2,1,0:T(1,128)}), f32[8,1,384]{2,1,0:T(1,128)S(1)}, u32[]{:S(2)}, u32[]{:S(2)}) async-start(f32[8,1,384]{2,1,0:T(1,128)} %copy.20), calls=%async_computation.2 | async-start | bytes 24576 | tf_op jit(solution)/shard_map/all_to_all | solution.py:91
  89.3 15.3 %pmax.7 = f32[4,1536]{1,0:T(4,128)S(1)} all-reduce(f32[4,1536]{1,0:T(4,128)S(1)} %get-tuple-element.19), channel_id=1, replica_groups=mesh['dp'=4,'expert'=8] {'dp'}, use_global_device_ids=true, to_apply=%region_3.4 | all-reduce | flops 6144 | bytes 49152 | tf_op jit(solution)/shard_map/pmax | solution.py:85
  104.5 0.6 dynamic-slice_bitcast_fusion
  105.1 0.6 gather_fusion.3
  105.7 0.7 bitcast_select_fusion
  (24 shorter events, 0.4 us)
Async XLA Ops:
  7.2 2.2 %copy-start.2 = (bf16[2,64,1536]{2,1,0:T(8,128)(2,1)S(1)}, bf16[2,64,1536]{2,1,0:T(8,128)(2,1)}, u32[]{:S(2)}) copy-start(bf16[2,64,1536]{2,1,0:T(8,128)(2,1)} %param.3) | copy-start | bytes 1179652
  9.5 2.7 %copy-start.1 = (bf16[2,64,1536]{2,1,0:T(8,128)(2,1)}, bf16[2,64,1536]{2,1,0:T(8,128)(2,1)S(1)}, u32[]{:S(2)}) copy-start(bf16[2,64,1536]{2,1,0:T(8,128)(2,1)S(1)} %multiply_convert_fusion) | copy-start | bytes 1179652
  12.1 44.2 %all-to-all-start = ((bf16[8,64,1536]{2,1,0:T(8,128)(2,1)}), bf16[8,64,1536]{2,1,0:T(8,128)(2,1)S(1)}, u32[]{:S(2)}, u32[]{:S(2)}) async-start(bf16[8,64,1536]{2,1,0:T(8,128)(2,1)} %copy.16), calls=%async_computation | async-start | bytes 3145728 | tf_op jit(solution)/shard_map/all_to_all | solution.py:40
  18.5 35.1 %all-gather.2.cloned.1.call-start = ((), (), s32[]{:S(2)}) async-start(), calls=%async_computation.3 | async-start | bytes 1966080 | tf_op jit(solution)/shard_map/all_gather | solution.py:37
  57.9 9.4 %copy-start = (bf16[2,256,1536]{2,1,0:T(8,128)(2,1)S(1)}, bf16[2,256,1536]{2,1,0:T(8,128)(2,1)}, u32[]{:S(2)}) copy-start(bf16[2,256,1536]{2,1,0:T(8,128)(2,1)} %all-gather.2.cloned.1.call-done) | copy-start | bytes 4718596
  63.0 14.4 %all-to-all-start.1 = ((bf16[4,2,49152]{2,1,0:T(2,128)(2,1)}), bf16[4,2,49152]{2,1,0:T(2,128)(2,1)S(1)}, u32[]{:S(2)}, u32[]{:S(2)}) async-start(bf16[4,2,49152]{2,1,0:T(2,128)(2,1)} %reshape.246), calls=%async_computation.1 | async-start | bytes 1572864 | tf_op jit(solution)/shard_map/all_to_all | solution.py:48
  85.4 19.7 %all-to-all-start.2 = ((f32[8,1,384]{2,1,0:T(1,128)}), f32[8,1,384]{2,1,0:T(1,128)S(1)}, u32[]{:S(2)}, u32[]{:S(2)}) async-start(f32[8,1,384]{2,1,0:T(1,128)} %copy.20), calls=%async_computation.2 | async-start | bytes 24576 | tf_op jit(solution)/shard_map/all_to_all | solution.py:91
Sparse Core Ops, SparseCore 0:
  21.1 32.4 all-gather.1
where the time goes:
time: 114 us; the launch traced here: 113 us
  waiting for transfers between devices  43.5 us (38%)
  local copies, waits for them, and re-layouts  16.8 us (15%)
  blocking collectives  15.3 us (13%)
  between operations  14.2 us (12%)
  starting transfers between devices  14 us (12%)
  matrix products  5.52 us (5%)
  other arithmetic  4 us (4%)
    all_gather x1, waiting for transfers between devices, body(): own_full = lax.all_gather(acts, 'dp', axis=1, tiled=True)  34.3 us
    pmax x1, blocking collectives, body(): left_all = lax.pmax(left_part, 'dp')  15.3 us
    all_to_all x1, waiting for transfers between devices, body(): lax.all_to_all(wanted, 'dp', split_axis=2, concat_axis=1, tiled=True)  7.57 us
    all_to_all x1, starting transfers between devices, body(): lax.all_to_all(outbound.reshape((num_devices,) + acts.shape[1:]), 'expert...  6.33 us
    dot_general x1, matrix products, single(): jnp.einsum('ra,rb->ab', left_rows, partner_block, preferred_element_type=...  4.63 us
    unnamed x10, local copies, waits for them, and re-layouts  4 us
    all_to_all x1, starting transfers between devices, body(): lax.all_to_all(outgoing, 'expert', split_axis=0, concat_axis=0, tiled=True)  3.88 us
    all_to_all x1, starting transfers between devices, body(): lax.all_to_all(wanted, 'dp', split_axis=2, concat_axis=1, tiled=True)  3.72 us
  transfers between devices with their start and end apart: 4, of which 3 were waited for; matrix products, arithmetic and copies ran while one was open for 5% of the time, Pallas kernels for 0%

commit v1 on v0

--- a/solution.py
+++ b/solution.py
@@ -1,14 +1,18 @@
+import functools
+import itertools
 import math
 
 import jax
 import jax.numpy as jnp
 from jax import lax
+from jax.experimental import pallas as pl
+from jax.experimental.pallas import tpu as pltpu
 from jax.sharding import PartitionSpec as P
 
 EPSILON = 1e-06
 
 
-def body(unit_codes, block_scales, pair_list):
+def general_body(unit_codes, block_scales, pair_list):
     num_devices = lax.axis_size("expert")
     groups = lax.axis_size("dp")
     my_index = lax.axis_index("expert")
@@ -95,6 +99,332 @@
     return (left_out[None], right_out[None])
 
 
+MESH = pl.DeviceIdType.MESH
+CHUNK = 256
+MAX_BRANCHES = 8
+TURNS = {
+    (1, 2, 4, 7): ((1, 7, 4, 2), (1, 1, 2, 2, 0, 3, 1, 0)),
+    (1, 3, 4, 7): ((1, 4, 7, 3), (0, 1, 3, 0, 3, 1, 2, 0)),
+    (1, 4, 5, 7): ((1, 4, 7, 5), (0, 0, 1, 3, 3, 2, 1, 2)),
+    (1, 4, 6, 7): ((1, 7, 6, 4), (0, 2, 1, 3, 2, 3, 3, 0)),
+}
+
+
+def pick(index, table):
+    total = 0
+    size = len(table)
+    for at, value in enumerate(table):
+        if value:
+            apart = (index - at) * (index - at)
+            total = total + value * (1 - (apart + size * size - 1) // (size * size))
+    return total
+
+
+def pair_kernel(
+    order, turns, n, groups,
+    codes_ref, scales_ref, pairs_ref, left_out, right_out,
+    acts, send_left, send_right, left_rows, right_rows, turned, inv_left, best, right_row,
+    left_stage, right_stage, left_got, right_got,
+    left_send_sem, left_sem, right_send_sem, right_sem, out_send_sem, left_got_sem, right_got_sem,
+):
+    me = lax.axis_index("expert")
+    dp = lax.axis_index("dp")
+    per_device, rows, units = codes_ref.shape
+    blocks = scales_ref.shape[1]
+    width = units // blocks
+    chunks = units // CHUNK
+    part = units // groups
+    all_rows = groups * rows
+
+    def share_of(member, column):
+        return (member - pick(column, turns) + groups) % groups
+
+    def member_of(share, column):
+        return (share + pick(column, turns)) % groups
+
+    mine = share_of(dp, me)
+    my_offset = pick(mine, order)
+    partner = (me + my_offset) % n
+    askers = [(me - order[k] + n) % n for k in range(groups)]
+    ask_member = [member_of(k, askers[k]) for k in range(groups)]
+    others = [(dp + r) % groups for r in range(1, groups)]
+
+    barrier = pltpu.get_barrier_semaphore()
+    greeted = [(other, me) for other in others]
+    greeted += [(ask_member[k], askers[k]) for k in range(groups)]
+    greeted += [(member, partner) for member in range(groups)]
+    for device in greeted:
+        pl.semaphore_signal(barrier, inc=1, device_id=device, device_id_type=MESH)
+
+    for expert in range(per_device):
+        factor = scales_ref[expert].T
+        for block in range(blocks):
+            at = slice(block * width, (block + 1) * width)
+            acts[expert, :, at] = (
+                codes_ref[expert, :, at].astype(jnp.float32) * factor[:, block : block + 1]
+            ).astype(jnp.bfloat16)
+
+    def slot_of(offset):
+        slot = 0
+        for s in range(groups):
+            slot = slot + jnp.where(pairs_ref[2 * s + 1] // per_device == offset, s, 0)
+        return slot
+
+    def chosen(column, slot, side):
+        return lax.rem(pairs_ref[2 * (groups * column + slot) + side], per_device)
+
+    for k in range(groups):
+        held = acts[chosen(askers[k], slot_of(order[k]), 1)]
+        for c in range(chunks):
+            send_right[k, c] = held[:, c * CHUNK : (c + 1) * CHUNK]
+    for r, other in enumerate(others):
+        offset = pick(share_of(other, me), order)
+        send_left[r] = acts[chosen(me, slot_of(offset), 0)]
+    my_rows = pl.ds(pl.multiple_of(dp * rows, rows), rows)
+    left_rows[my_rows, :] = acts[chosen(me, slot_of(my_offset), 0)]
+
+    def left_copy(r):
+        return pltpu.make_async_remote_copy(
+            src_ref=send_left.at[r],
+            dst_ref=left_rows.at[my_rows, :],
+            send_sem=left_send_sem.at[r],
+            recv_sem=left_sem.at[dp],
+            device_id=(others[r], me),
+            device_id_type=MESH,
+        )
+
+    def right_copy(k, c):
+        return pltpu.make_async_remote_copy(
+            src_ref=send_right.at[k, c],
+            dst_ref=right_rows.at[c, my_rows, :],
+            send_sem=right_send_sem.at[k, c],
+            recv_sem=right_sem.at[c, dp],
+            device_id=(ask_member[k], askers[k]),
+            device_id_type=MESH,
+        )
+
+    pl.semaphore_wait(barrier, len(greeted))
+    for r in range(groups - 1):
+        left_copy(r).start()
+
+    @pl.loop(0, chunks)
+    def _(c):
+        for k in range(groups):
+            right_copy(k, c).start()
+
+    best[...] = jnp.full_like(best, -jnp.inf)
+    for other in others:
+        theirs = pl.ds(pl.multiple_of(other * rows, rows), rows)
+        pltpu.make_async_remote_copy(
+            src_ref=send_left.at[0],
+            dst_ref=left_rows.at[theirs, :],
+            send_sem=left_send_sem.at[0],
+            recv_sem=left_sem.at[other],
+            device_id=(other, me),
+            device_id_type=MESH,
+        ).wait_recv()
+
+    for i in range(chunks):
+        at = slice(i * CHUNK, (i + 1) * CHUNK)
+        block = left_rows[:, at]
+        wide = block.astype(jnp.float32)
+        square = jnp.sum(wide * wide, axis=0, keepdims=True) / all_rows
+        inverse = 1.0 / jnp.sqrt(square + EPSILON)
+        inv_left[at, :] = jnp.broadcast_to(inverse, (128, CHUNK)).T
+        turned[at, :] = block.T
+
+    @pl.loop(0, chunks)
+    def _(c):
+        for member in range(groups):
+            pltpu.make_async_remote_copy(
+                src_ref=send_right.at[0, 0],
+                dst_ref=right_rows.at[c, pl.ds(member * rows, rows), :],
+                send_sem=right_send_sem.at[0, 0],
+                recv_sem=right_sem.at[c, member],
+                device_id=(member, partner),
+                device_id_type=MESH,
+            ).wait_recv()
+        block = right_rows[c]
+        wide = block.astype(jnp.float32)
+        square = jnp.sum(wide * wide, axis=0, keepdims=True) / all_rows
+        inverse = 1.0 / jnp.sqrt(square + EPSILON)
+        tops = [jnp.full((8, 128), -jnp.inf, jnp.float32) for _ in range(CHUNK // 128)]
+        for i in range(chunks):
+            at = slice(i * CHUNK, (i + 1) * CHUNK)
+            gram = jnp.dot(turned[at, :], block, preferred_element_type=jnp.float32)
+            scale = inv_left[at, :]
+            running = best[at, :]
+            for h in range(CHUNK // 128):
+                lanes = slice(h * 128, (h + 1) * 128)
+                scaled = gram[:, lanes] * scale
+                running = jnp.maximum(running, scaled * inverse[:, lanes])
+                gram_top = jnp.max(scaled.reshape(CHUNK // 8, 8, 128), axis=0)
+                tops[h] = jnp.maximum(tops[h], gram_top)
+            best[at, :] = running
+        top = jnp.max(jnp.concatenate(tops, axis=1), axis=0, keepdims=True)
+        right_row[c] = top * inverse / all_rows
+
+    right_full = jnp.concatenate([right_row[c] for c in range(chunks)], axis=1)
+    left_full = jnp.concatenate(
+        [
+            jnp.max(best[i * CHUNK : (i + 1) * CHUNK, :].T, axis=0, keepdims=True)
+            for i in range(chunks)
+        ],
+        axis=1,
+    ) / all_rows
+    for member in range(groups):
+        at = slice(member * part, (member + 1) * part)
+        right_stage[member] = right_full[:, at]
+        left_stage[member] = left_full[:, at]
+
+    def right_result(member):
+        return pltpu.make_async_remote_copy(
+            src_ref=right_stage.at[member],
+            dst_ref=right_got.at[mine],
+            send_sem=out_send_sem.at[member],
+            recv_sem=right_got_sem.at[mine],
+            device_id=(member, partner),
+            device_id_type=MESH,
+        )
+
+    def left_result(r):
+        return pltpu.make_async_remote_copy(
+            src_ref=left_stage.at[others[r]],
+            dst_ref=left_got.at[mine],
+            send_sem=out_send_sem.at[groups + r],
+            recv_sem=left_got_sem.at[mine],
+            device_id=(others[r], me),
+            device_id_type=MESH,
+        )
+
+    for member in range(groups):
+        right_result(member).start()
+    for r in range(groups - 1):
+        left_result(r).start()
+    left_got[mine] = left_stage[dp]
+
+    for r in range(groups - 1):
+        left_copy(r).wait_send()
+
+    @pl.loop(0, chunks)
+    def _(c):
+        for k in range(groups):
+            right_copy(k, c).wait_send()
+
+    for other in others:
+        share = share_of(other, me)
+        pltpu.make_async_remote_copy(
+            src_ref=left_stage.at[0],
+            dst_ref=left_got.at[share],
+            send_sem=out_send_sem.at[0],
+            recv_sem=left_got_sem.at[share],
+            device_id=(other, me),
+            device_id_type=MESH,
+        ).wait_recv()
+    for k in range(groups):
+        pltpu.make_async_remote_copy(
+            src_ref=right_stage.at[0],
+            dst_ref=right_got.at[k],
+            send_sem=out_send_sem.at[0],
+            recv_sem=right_got_sem.at[k],
+            device_id=(ask_member[k], askers[k]),
+            device_id_type=MESH,
+        ).wait_recv()
+    for member in range(groups):
+        right_result(member).wait_send()
+    for r in range(groups - 1):
+        left_result(r).wait_send()
+
+    for s in range(groups):
+        offset = pairs_ref[2 * s + 1] // per_device
+        share = 0
+        for k in range(groups):
+            share = share + jnp.where(offset == order[k], k, 0)
+        left_out[0, s : s + 1, :] = left_got[share]
+        right_out[0, s : s + 1, :] = right_got[share]
+
+
+def pair_call(order, turns, n, groups, collective_id, unit_codes, block_scales, pairs):
+    per_device, rows, units = unit_codes.shape
+    chunks = units // CHUNK
+    part = units // groups
+    out = jax.ShapeDtypeStruct((1, groups, part), jnp.float32)
+    vmem = pl.BlockSpec(memory_space=pltpu.VMEM)
+    dma = pltpu.SemaphoreType.DMA
+    return pl.pallas_call(
+        functools.partial(pair_kernel, order, turns, n, groups),
+        out_shape=(out, out),
+        in_specs=[vmem, vmem, pl.BlockSpec(memory_space=pltpu.SMEM)],
+        out_specs=(vmem, vmem),
+        scratch_shapes=[
+            pltpu.VMEM((per_device, rows, units), jnp.bfloat16),
+            pltpu.VMEM((groups - 1, rows, units), jnp.bfloat16),
+            pltpu.VMEM((groups, chunks, rows, CHUNK), jnp.bfloat16),
+            pltpu.VMEM((groups * rows, units), jnp.bfloat16),
+            pltpu.VMEM((chunks, groups * rows, CHUNK), jnp.bfloat16),
+            pltpu.VMEM((units, groups * rows), jnp.bfloat16),
+            pltpu.VMEM((units, 128), jnp.float32),
+            pltpu.VMEM((units, 128), jnp.float32),
+            pltpu.VMEM((chunks, 1, CHUNK), jnp.float32),
+            pltpu.VMEM((groups, 1, part), jnp.float32),
+            pltpu.VMEM((groups, 1, part), jnp.float32),
+            pltpu.VMEM((groups, 1, part), jnp.float32),
+            pltpu.VMEM((groups, 1, part), jnp.float32),
+            dma((groups - 1,)),
+            dma((groups,)),
+            dma((groups, chunks)),
+            dma((chunks, groups)),
+            dma((2 * groups - 1,)),
+            dma((groups,)),
+            dma((groups,)),
+        ],
+        compiler_params=pltpu.CompilerParams(
+            collective_id=collective_id, has_side_effects=True, vmem_limit_bytes=24 * 2**20
+        ),
+        cost_estimate=pl.CostEstimate(
+            flops=2 * units * units * groups * rows, bytes_accessed=2 * units * rows * per_device, transcendentals=0
+        ),
+    )(unit_codes, block_scales, pairs)
+
+
+def offset_sets(n, slots):
+    fixed = sorted({1, n // 2, n - 1})
+    rest = [o for o in range(1, n) if o not in fixed]
+    free = slots - len(fixed)
+    if free < 0 or math.comb(len(rest), free) > MAX_BRANCHES:
+        return []
+    return [tuple(sorted(fixed + list(more))) for more in itertools.combinations(rest, free)]
+
+
+def body(unit_codes, block_scales, pair_list):
+    n = lax.axis_size("expert")
+    groups = lax.axis_size("dp")
+    per_device, rows, units = unit_codes.shape
+    slots = pair_list.shape[0] // n
+    sets = offset_sets(n, slots)
+    fits = (
+        slots == groups
+        and rows % 16 == 0
+        and units % CHUNK == 0
+        and units % (128 * groups) == 0
+        and (groups * rows) % 128 == 0
+    )
+    if not sets or not fits:
+        return general_body(unit_codes, block_scales, pair_list)
+    offsets = pair_list[:slots, 1] // per_device
+    branch = 0
+    for at, members in enumerate(sets):
+        same = sum(members) == jnp.sum(offsets)
+        if len({sum(m) for m in sets}) < len(sets):
+            same = jnp.all(jnp.any(offsets[:, None] == jnp.asarray(members)[None, :], axis=1))
+        branch = branch + jnp.where(same, at, 0)
+    calls = []
+    for at, members in enumerate(sets):
+        order, turns = TURNS.get(members, (members, (0,) * n)) if (n, groups) == (8, 4) else (members, (0,) * n)
+        calls.append(functools.partial(pair_call, order, turns, n, groups, at))
+    return lax.switch(branch, calls, unit_codes, block_scales, pair_list.reshape(-1))
+
+
 def solution(mesh):
     in_specs = (P("expert", "dp", None), P("expert", None, "dp"), P())
     out_specs = (P("expert", None, "dp"), P("expert", None, "dp"))

time: 114 us -> 38.4 us (0.34)
  waiting for transfers between devices: 43.5 us -> 0 us
  Pallas kernels: 0 us -> 32.1 us
  blocking collectives: 15.3 us -> 0 us
  local copies, waits for them, and re-layouts: 16.8 us -> 2.05 us
  starting transfers between devices: 14 us -> 0 us
  between operations: 14.2 us -> 2.62 us
  matrix products: 5.52 us -> 0 us
  other arithmetic: 4 us -> 1.33 us
    all_gather x1 -> x0, waiting for transfers between devices: 34.3 us -> none  [body(): own_full = lax.all_gather(acts, 'dp', axis=1, tiled=True)]
    pallas_call x0 -> x1, Pallas kernels: none -> 32.1 us  [pair_call(): pl.pallas_call(functools.partial(pair_kernel, order, turns, n, groups), o...]
    pmax x1 -> x0, blocking collectives: 15.3 us -> none  [body(): left_all = lax.pmax(left_part, 'dp')]
    all_to_all x3 -> x0, starting transfers between devices: 13.9 us -> none  [the longest x1 6.33 us: body(): lax.all_to_all(outbound.reshape((num_devices,) + acts.shape[1:]), 'expert...]
    all_to_all x3 -> x0, waiting for transfers between devices: 8.5 us -> none  [the longest x1 7.57 us: body(): lax.all_to_all(wanted, 'dp', split_axis=2, concat_axis=1, tiled=True)]
    dot_general x3 -> x0, matrix products: 5.52 us -> none  [the longest x1 4.63 us: single(): jnp.einsum('ra,rb->ab', left_rows, partner_block, preferred_element_type=...]
    gather x4 -> x0, local copies, waits for them, and re-layouts: 4.14 us -> none  [the longest x1 2.41 us: single(): left_rows = jnp.take(own_full, expert_pick, axis=0)]
    select_n x1 -> x0, local copies, waits for them, and re-layouts: 2.66 us -> none  [body(): wanted = jnp.take(received, right_dev, axis=0)]
  transfers between devices with their start and end apart: 4 -> 0, of which waited for: 3 -> 0; matrix products, arithmetic and copies ran while one was open for 5% -> 0% of each run, Pallas kernels for 0% -> 0%
where the time goes in v1:
time: 38.4 us; the launch traced here: 38.1 us
  Pallas kernels  32.1 us (84%)
  between operations  2.62 us (7%)
  local copies, waits for them, and re-layouts  2.05 us (5%)
  other arithmetic  1.33 us (3%)
    pallas_call x1, Pallas kernels, pair_call(): pl.pallas_call(functools.partial(pair_kernel, order, turns, n, groups), o...  32.1 us
    unnamed x6, local copies, waits for them, and re-layouts  1.85 us
    reduce_sum x1, other arithmetic, body(): same = sum(members) == jnp.sum(offsets)  1.33 us

profile of v1, /device:TPU:0, one launch (start us, length us, event | category | flops | bytes accessed | tf_op | source)
XLA Modules:
  0.0 38.1 jit_solution(4071277144859438268)
XLA Ops:
  0.6 0.0 copy-start
  0.6 1.3 %fusion = s32[]{:T(128)} fusion(s32[32,2]{0,1:T(2,128)} %param.9), kind=kLoop, calls=%fused_computation.5 | loop fusion | flops 63 | bytes 20 | tf_op jit(solution)/shard_map/reduce_sum | solution.py:417
  3.9 0.0 copy-start.1
  3.9 0.0 copy-done
  3.9 0.7 %copy-done.1 = s32[32,2]{0,1:T(2,128)S(1)} copy-done((s32[32,2]{0,1:T(2,128)S(1)}, s32[32,2]{0,1:T(2,128)}, u32[]{:S(2)}) %copy-start.1) | copy-done | bytes 280
  4.6 32.3 %conditional.1 = ((f32[1,4,384]{2,1,0:T(4,128)S(1)}, f32[1,4,384]{2,1,0:T(4,128)S(1)})) conditional(s32[]{:T(128)} %clamp.3, (bf16[2,64,1536]{2,1,0:T(8,128)(2,1)}, f32[2,12,64]{2,0,1:T(2,128)S(1)}, s32[32,2]{0,1:T(2,128)S(1)}) %tuple.50, (bf16[2,64,1536]{2,1,0:T(8,128)(2,1)}, f32[2,12,64]{2,0,1:T(2,128)S(1)}, ...), branch_computations={%region_1.2_spmd, %region_2.3_spmd, %region_3.4_spmd, %region_4.5_... | conditional | flops 1207959552 | bytes 406536 | solution.py:425
  4.6 0.1 copy.36
  4.7 0.1 reshape.11.pairs_ref
  4.8 32.1 %branch_3_fun.1 = (f32[1,4,384]{2,1,0:T(4,128)S(1)}, f32[1,4,384]{2,1,0:T(4,128)S(1)}) custom-call(bf16[2,64,1536]{2,1,0:T(8,128)(2,1)} %get-tuple-element.63.codes_ref, f32[2,12,64]{2,1,0:T(8,128)S(1)} %copy.35.scales_ref, s32[64]{0:T(128)S(1)} %reshape.11.pairs_ref), custom_call_target="tpu_custom_call" | custom-call | flops 1207959552 | bytes 393216 | tf_op jit(solution)/shard_map/cond/branch_3_fun/pallas_call | solution.py:354
  36.9 0.6 %copy.47 = f32[1,4,384]{2,1,0:T(4,128)} copy(f32[1,4,384]{2,1,0:T(4,128)S(1)} %get-tuple-element.102) | data formatting | bytes 12288
  37.5 0.6 %copy.48 = f32[1,4,384]{2,1,0:T(4,128)} copy(f32[1,4,384]{2,1,0:T(4,128)S(1)} %get-tuple-element.103) | data formatting | bytes 12288
  (1 shorter events, 0.0 us)
Async XLA Ops:
  0.6 3.3 %copy-start = (f32[2,12,64]{2,0,1:T(2,128)S(1)}, f32[2,12,64]{2,0,1:T(2,128)}, u32[]{:S(2)}) copy-start(f32[2,12,64]{2,0,1:T(2,128)} %param.8) | copy-start | bytes 18436
  3.9 0.7 %copy-start.1 = (s32[32,2]{0,1:T(2,128)S(1)}, s32[32,2]{0,1:T(2,128)}, u32[]{:S(2)}) copy-start(s32[32,2]{0,1:T(2,128)} %param.9) | copy-start | bytes 772

commit v2 on v1

--- a/solution.py
+++ b/solution.py
@@ -167,11 +167,11 @@
     def slot_of(offset):
         slot = 0
         for s in range(groups):
-            slot = slot + jnp.where(pairs_ref[2 * s + 1] // per_device == offset, s, 0)
+            slot = slot + jnp.where(pairs_ref[1, s] // per_device == offset, s, 0)
         return slot
 
     def chosen(column, slot, side):
-        return lax.rem(pairs_ref[2 * (groups * column + slot) + side], per_device)
+        return lax.rem(pairs_ref[side, groups * column + slot], per_device)
 
     for k in range(groups):
         held = acts[chosen(askers[k], slot_of(order[k]), 1)]
@@ -179,16 +179,20 @@
             send_right[k, c] = held[:, c * CHUNK : (c + 1) * CHUNK]
     for r, other in enumerate(others):
         offset = pick(share_of(other, me), order)
-        send_left[r] = acts[chosen(me, slot_of(offset), 0)]
+        held = acts[chosen(me, slot_of(offset), 0)]
+        for c in range(chunks):
+            send_left[r, c] = held[:, c * CHUNK : (c + 1) * CHUNK]
     my_rows = pl.ds(pl.multiple_of(dp * rows, rows), rows)
-    left_rows[my_rows, :] = acts[chosen(me, slot_of(my_offset), 0)]
-
-    def left_copy(r):
+    held = acts[chosen(me, slot_of(my_offset), 0)]
+    for c in range(chunks):
+        left_rows[c, my_rows, :] = held[:, c * CHUNK : (c + 1) * CHUNK]
+
+    def left_copy(r, c):
         return pltpu.make_async_remote_copy(
-            src_ref=send_left.at[r],
-            dst_ref=left_rows.at[my_rows, :],
-            send_sem=left_send_sem.at[r],
-            recv_sem=left_sem.at[dp],
+            src_ref=send_left.at[r, c],
+            dst_ref=left_rows.at[c, my_rows, :],
+            send_sem=left_send_sem.at[r, c],
+            recv_sem=left_sem.at[c, dp],
             device_id=(others[r], me),
             device_id_type=MESH,
         )
@@ -204,29 +208,29 @@
         )
 
     pl.semaphore_wait(barrier, len(greeted))
-    for r in range(groups - 1):
-        left_copy(r).start()
-
-    @pl.loop(0, chunks)
-    def _(c):
+    ahead = (2 * chunks + 2) // 3
+    for c in range(chunks):
         for k in range(groups):
             right_copy(k, c).start()
+        if c < ahead:
+            for at in range(c * chunks // ahead, (c + 1) * chunks // ahead):
+                for r in range(groups - 1):
+                    left_copy(r, at).start()
 
     best[...] = jnp.full_like(best, -jnp.inf)
-    for other in others:
-        theirs = pl.ds(pl.multiple_of(other * rows, rows), rows)
-        pltpu.make_async_remote_copy(
-            src_ref=send_left.at[0],
-            dst_ref=left_rows.at[theirs, :],
-            send_sem=left_send_sem.at[0],
-            recv_sem=left_sem.at[other],
-            device_id=(other, me),
-            device_id_type=MESH,
-        ).wait_recv()
-
     for i in range(chunks):
         at = slice(i * CHUNK, (i + 1) * CHUNK)
-        block = left_rows[:, at]
+        for other in others:
+            theirs = pl.ds(pl.multiple_of(other * rows, rows), rows)
+            pltpu.make_async_remote_copy(
+                src_ref=send_left.at[0, 0],
+                dst_ref=left_rows.at[i, theirs, :],
+                send_sem=left_send_sem.at[0, 0],
+                recv_sem=left_sem.at[i, other],
+                device_id=(other, me),
+                device_id_type=MESH,
+            ).wait_recv()
+        block = left_rows[i]
         wide = block.astype(jnp.float32)
         square = jnp.sum(wide * wide, axis=0, keepdims=True) / all_rows
         inverse = 1.0 / jnp.sqrt(square + EPSILON)
@@ -303,11 +307,10 @@
         left_result(r).start()
     left_got[mine] = left_stage[dp]
 
-    for r in range(groups - 1):
-        left_copy(r).wait_send()
-
     @pl.loop(0, chunks)
     def _(c):
+        for r in range(groups - 1):
+            left_copy(r, c).wait_send()
         for k in range(groups):
             right_copy(k, c).wait_send()
 
@@ -336,7 +339,7 @@
         left_result(r).wait_send()
 
     for s in range(groups):
-        offset = pairs_ref[2 * s + 1] // per_device
+        offset = pairs_ref[1, s] // per_device
         share = 0
         for k in range(groups):
             share = share + jnp.where(offset == order[k], k, 0)
@@ -358,9 +361,9 @@
         out_specs=(vmem, vmem),
         scratch_shapes=[
             pltpu.VMEM((per_device, rows, units), jnp.bfloat16),
-            pltpu.VMEM((groups - 1, rows, units), jnp.bfloat16),
+            pltpu.VMEM((groups - 1, chunks, rows, CHUNK), jnp.bfloat16),
             pltpu.VMEM((groups, chunks, rows, CHUNK), jnp.bfloat16),
-            pltpu.VMEM((groups * rows, units), jnp.bfloat16),
+            pltpu.VMEM((chunks, groups * rows, CHUNK), jnp.bfloat16),
             pltpu.VMEM((chunks, groups * rows, CHUNK), jnp.bfloat16),
             pltpu.VMEM((units, groups * rows), jnp.bfloat16),
             pltpu.VMEM((units, 128), jnp.float32),
@@ -370,8 +373,8 @@
             pltpu.VMEM((groups, 1, part), jnp.float32),
             pltpu.VMEM((groups, 1, part), jnp.float32),
             pltpu.VMEM((groups, 1, part), jnp.float32),
-            dma((groups - 1,)),
-            dma((groups,)),
+            dma((groups - 1, chunks)),
+            dma((chunks, groups)),
             dma((groups, chunks)),
             dma((chunks, groups)),
             dma((2 * groups - 1,)),
@@ -412,17 +415,19 @@
     if not sets or not fits:
         return general_body(unit_codes, block_scales, pair_list)
     offsets = pair_list[:slots, 1] // per_device
-    branch = 0
-    for at, members in enumerate(sets):
-        same = sum(members) == jnp.sum(offsets)
-        if len({sum(m) for m in sets}) < len(sets):
+    if slots == 4 and n > 4:
+        free = [(sum(members) - 1 - n // 2 - (n - 1), at) for at, members in enumerate(sets)]
+        branch = jnp.sum(sum(jnp.where(offsets == offset, at, 0) for offset, at in free))
+    else:
+        branch = 0
+        for at, members in enumerate(sets):
             same = jnp.all(jnp.any(offsets[:, None] == jnp.asarray(members)[None, :], axis=1))
-        branch = branch + jnp.where(same, at, 0)
+            branch = branch + jnp.where(same, at, 0)
     calls = []
     for at, members in enumerate(sets):
         order, turns = TURNS.get(members, (members, (0,) * n)) if (n, groups) == (8, 4) else (members, (0,) * n)
         calls.append(functools.partial(pair_call, order, turns, n, groups, at))
-    return lax.switch(branch, calls, unit_codes, block_scales, pair_list.reshape(-1))
+    return lax.switch(branch, calls, unit_codes, block_scales, pair_list.T)
 
 
 def solution(mesh):

time: 38.4 us -> 38.4 us (level); the launches traced: 38.1 us -> 39 us
  Pallas kernels: 32.1 us -> 33.8 us
  between operations: 2.62 us -> 1.3 us
  local copies, waits for them, and re-layouts: 2.05 us -> 2.57 us
    pallas_call x1, Pallas kernels: 32.1 us -> 33.8 us  [pair_call(): pl.pallas_call(functools.partial(pair_kernel, order, turns, n, groups), o...]
    another operation x2 -> x1, local copies, waits for them, and re-layouts: 0.09 us -> 0.71 us
    unnamed x6 -> x4, local copies, waits for them, and re-layouts: 1.85 us -> 1.86 us
where the time goes in v2:
time: 38.4 us; the launch traced here: 39 us
  Pallas kernels  33.8 us (88%)
  local copies, waits for them, and re-layouts  2.57 us (7%)
  other arithmetic  1.33 us (3%)
  between operations  1.3 us (3%)
    pallas_call x1, Pallas kernels, pair_call(): pl.pallas_call(functools.partial(pair_kernel, order, turns, n, groups), o...  33.8 us
    unnamed x4, local copies, waits for them, and re-layouts  1.86 us
    reduce_sum x1, other arithmetic, body(): jnp.sum(sum((jnp.where(offsets == offset, at, 0) for offset, at in free)))  1.33 us

profile of v2, /device:TPU:0, one launch (start us, length us, event | category | flops | bytes accessed | tf_op | source)
XLA Modules:
  0.0 39.0 jit_solution(12994456093506044087)
XLA Ops:
  0.6 1.3 %fusion.2 = s32[]{:T(128)} fusion(s32[32,2]{0,1:T(2,128)} %param.9), kind=kLoop, calls=%fused_computation.9 | loop fusion | flops 95 | bytes 20 | tf_op jit(solution)/shard_map/reduce_sum | solution.py:420
  2.6 0.0 copy-start
  2.6 0.7 %copy-done = s32[32,2]{0,1:T(2,128)S(1)} copy-done((s32[32,2]{0,1:T(2,128)S(1)}, s32[32,2]{0,1:T(2,128)}, u32[]{:S(2)}) %copy-start) | copy-done | bytes 280
  3.3 34.5 %conditional.1 = ((f32[1,4,384]{2,1,0:T(4,128)S(1)}, f32[1,4,384]{2,1,0:T(4,128)S(1)})) conditional(s32[]{:T(128)} %clamp.3, (bf16[2,64,1536]{2,1,0:T(8,128)(2,1)}, f32[2,12,64]{2,0,1:T(2,128)}, s32[2,32]{1,0:T(2,128)S(1)}) %tuple.42, (bf16[2,64,1536]{2,1,0:T(8,128)(2,1)}, f32[2,12,64]{2,0,1:T(2,128)}, ...), branch_computations={%region_1.2_spmd, %region_2.3_spmd, %region_3.4_spmd, %region_4.5_... | conditional | flops 1207959552 | bytes 405512 | solution.py:430
  3.3 0.7 %copy.23.scales_ref = f32[2,12,64]{2,1,0:T(8,128)S(1)} copy(f32[2,12,64]{2,0,1:T(2,128)} %get-tuple-element.71) | data formatting | bytes 12288 | tf_op jit(solution)/shard_map
  4.0 33.8 %branch_2_fun.1 = (f32[1,4,384]{2,1,0:T(4,128)S(1)}, f32[1,4,384]{2,1,0:T(4,128)S(1)}) custom-call(bf16[2,64,1536]{2,1,0:T(8,128)(2,1)} %get-tuple-element.58.codes_ref, f32[2,12,64]{2,1,0:T(8,128)S(1)} %copy.23.scales_ref, s32[2,32]{1,0:T(2,128)S(1)} %get-tuple-element.32.pairs_ref), custom_call_target="tpu_custom_call" | custom-call | flops 1207959552 | bytes 393216 | tf_op jit(solution)/shard_map/cond/branch_2_fun/pallas_call | solution.py:357
  37.8 0.6 %copy.35 = f32[1,4,384]{2,1,0:T(4,128)} copy(f32[1,4,384]{2,1,0:T(4,128)S(1)} %get-tuple-element.86) | data formatting | bytes 12288
  38.4 0.6 %copy.36 = f32[1,4,384]{2,1,0:T(4,128)} copy(f32[1,4,384]{2,1,0:T(4,128)S(1)} %get-tuple-element.87) | data formatting | bytes 12288
Async XLA Ops:
  2.6 0.7 %copy-start = (s32[32,2]{0,1:T(2,128)S(1)}, s32[32,2]{0,1:T(2,128)}, u32[]{:S(2)}) copy-start(s32[32,2]{0,1:T(2,128)} %param.9) | copy-start | bytes 772

commit v3 on v2

--- a/solution.py
+++ b/solution.py
@@ -123,14 +123,14 @@
 def pair_kernel(
     order, turns, n, groups,
     codes_ref, scales_ref, pairs_ref, left_out, right_out,
-    acts, send_left, send_right, left_rows, right_rows, turned, inv_left, best, right_row,
+    codes, acts, send_left, send_right, left_rows, right_rows, turned, inv_left, best, right_row,
     left_stage, right_stage, left_got, right_got,
-    left_send_sem, left_sem, right_send_sem, right_sem, out_send_sem, left_got_sem, right_got_sem,
+    load_sem, left_send_sem, left_sem, right_send_sem, right_sem, out_send_sem, left_got_sem, right_got_sem,
 ):
     me = lax.axis_index("expert")
     dp = lax.axis_index("dp")
     per_device, rows, units = codes_ref.shape
-    blocks = scales_ref.shape[1]
+    blocks = scales_ref.shape[0]
     width = units // blocks
     chunks = units // CHUNK
     part = units // groups
@@ -156,13 +156,8 @@
     for device in greeted:
         pl.semaphore_signal(barrier, inc=1, device_id=device, device_id_type=MESH)
 
-    for expert in range(per_device):
-        factor = scales_ref[expert].T
-        for block in range(blocks):
-            at = slice(block * width, (block + 1) * width)
-            acts[expert, :, at] = (
-                codes_ref[expert, :, at].astype(jnp.float32) * factor[:, block : block + 1]
-            ).astype(jnp.bfloat16)
+    load = pltpu.make_async_copy(codes_ref, codes, load_sem)
+    load.start()
 
     def slot_of(offset):
         slot = 0
@@ -173,19 +168,26 @@
     def chosen(column, slot, side):
         return lax.rem(pairs_ref[side, groups * column + slot], per_device)
 
-    for k in range(groups):
-        held = acts[chosen(askers[k], slot_of(order[k]), 1)]
-        for c in range(chunks):
-            send_right[k, c] = held[:, c * CHUNK : (c + 1) * CHUNK]
-    for r, other in enumerate(others):
-        offset = pick(share_of(other, me), order)
-        held = acts[chosen(me, slot_of(offset), 0)]
-        for c in range(chunks):
-            send_left[r, c] = held[:, c * CHUNK : (c + 1) * CHUNK]
     my_rows = pl.ds(pl.multiple_of(dp * rows, rows), rows)
-    held = acts[chosen(me, slot_of(my_offset), 0)]
-    for c in range(chunks):
-        left_rows[c, my_rows, :] = held[:, c * CHUNK : (c + 1) * CHUNK]
+    right_pick = [chosen(askers[k], slot_of(order[k]), 1) for k in range(groups)]
+    left_pick = [
+        chosen(me, slot_of(pick(share_of(member, me), order)), 0) for member in others + [dp]
+    ]
+    factors = [scales_ref[:, expert, :].T for expert in range(per_device)]
+
+    def scale_and_stage(c):
+        for expert in range(per_device):
+            for block in range(c * CHUNK // width, (c + 1) * CHUNK // width):
+                at = slice(block * width, (block + 1) * width)
+                inside = slice(block * width - c * CHUNK, (block + 1) * width - c * CHUNK)
+                acts[expert, c, :, inside] = (
+                    codes[expert, :, at].astype(jnp.float32) * factors[expert][:, block : block + 1]
+                ).astype(jnp.bfloat16)
+        for k in range(groups):
+            send_right[k, c] = acts[right_pick[k], c]
+        for r in range(groups - 1):
+            send_left[r, c] = acts[left_pick[r], c]
+        left_rows[c, my_rows, :] = acts[left_pick[-1], c]
 
     def left_copy(r, c):
         return pltpu.make_async_remote_copy(
@@ -207,15 +209,21 @@
             device_id_type=MESH,
         )
 
-    pl.semaphore_wait(barrier, len(greeted))
+    load.wait()
     ahead = (2 * chunks + 2) // 3
+    staged = 0
     for c in range(chunks):
+        lefts = range(c * chunks // ahead, (c + 1) * chunks // ahead) if c < ahead else range(0)
+        while staged <= max([c, *lefts]):
+            scale_and_stage(staged)
+            staged += 1
+        if c == 0:
+            pl.semaphore_wait(barrier, len(greeted))
         for k in range(groups):
             right_copy(k, c).start()
-        if c < ahead:
-            for at in range(c * chunks // ahead, (c + 1) * chunks // ahead):
-                for r in range(groups - 1):
-                    left_copy(r, at).start()
+        for at in lefts:
+            for r in range(groups - 1):
+                left_copy(r, at).start()
 
     best[...] = jnp.full_like(best, -jnp.inf)
     for i in range(chunks):
@@ -357,10 +365,11 @@
     return pl.pallas_call(
         functools.partial(pair_kernel, order, turns, n, groups),
         out_shape=(out, out),
-        in_specs=[vmem, vmem, pl.BlockSpec(memory_space=pltpu.SMEM)],
+        in_specs=[pl.BlockSpec(memory_space=pl.ANY), vmem, pl.BlockSpec(memory_space=pltpu.SMEM)],
         out_specs=(vmem, vmem),
         scratch_shapes=[
             pltpu.VMEM((per_device, rows, units), jnp.bfloat16),
+            pltpu.VMEM((per_device, chunks, rows, CHUNK), jnp.bfloat16),
             pltpu.VMEM((groups - 1, chunks, rows, CHUNK), jnp.bfloat16),
             pltpu.VMEM((groups, chunks, rows, CHUNK), jnp.bfloat16),
             pltpu.VMEM((chunks, groups * rows, CHUNK), jnp.bfloat16),
@@ -373,6 +382,7 @@
             pltpu.VMEM((groups, 1, part), jnp.float32),
             pltpu.VMEM((groups, 1, part), jnp.float32),
             pltpu.VMEM((groups, 1, part), jnp.float32),
+            dma,
             dma((groups - 1, chunks)),
             dma((chunks, groups)),
             dma((groups, chunks)),
@@ -382,12 +392,12 @@
             dma((groups,)),
         ],
         compiler_params=pltpu.CompilerParams(
-            collective_id=collective_id, has_side_effects=True, vmem_limit_bytes=24 * 2**20
+            collective_id=collective_id, has_side_effects=True, vmem_limit_bytes=56 * 2**20
         ),
         cost_estimate=pl.CostEstimate(
             flops=2 * units * units * groups * rows, bytes_accessed=2 * units * rows * per_device, transcendentals=0
         ),
-    )(unit_codes, block_scales, pairs)
+    )(unit_codes, jnp.transpose(block_scales, (1, 0, 2)), pairs)
 
 
 def offset_sets(n, slots):
@@ -409,6 +419,8 @@
         slots == groups
         and rows % 16 == 0
         and units % CHUNK == 0
+        and CHUNK % (units // block_scales.shape[1]) == 0
+        and units // block_scales.shape[1] % 128 == 0
         and units % (128 * groups) == 0
         and (groups * rows) % 128 == 0
     )

time: 38.4 us -> 37.6 us (0.979)
  local copies, waits for them, and re-layouts: 2.57 us -> 1.86 us
    another operation x1 -> x0, local copies, waits for them, and re-layouts: 0.71 us -> none
where the time goes in v3:
time: 37.6 us; the launch traced here: 38 us
  Pallas kernels  33.5 us (89%)
  local copies, waits for them, and re-layouts  1.86 us (5%)
  other arithmetic  1.33 us (4%)
  between operations  1.3 us (3%)
    pallas_call x1, Pallas kernels, pair_call(): pl.pallas_call(functools.partial(pair_kernel, order, turns, n, groups), o...  33.5 us
    unnamed x4, local copies, waits for them, and re-layouts  1.86 us
    reduce_sum x1, other arithmetic, body(): jnp.sum(sum((jnp.where(offsets == offset, at, 0) for offset, at in free)))  1.33 us

profile of v3, /device:TPU:0, one launch (start us, length us, event | category | flops | bytes accessed | tf_op | source)
XLA Modules:
  0.0 38.0 jit_solution(16395477958838762935)
XLA Ops:
  0.6 1.3 %fusion.2 = s32[]{:T(128)} fusion(s32[32,2]{0,1:T(2,128)} %param.9), kind=kLoop, calls=%fused_computation.9 | loop fusion | flops 95 | bytes 20 | tf_op jit(solution)/shard_map/reduce_sum | solution.py:432
  2.6 0.0 copy-start
  2.6 0.7 %copy-done = s32[32,2]{0,1:T(2,128)S(1)} copy-done((s32[32,2]{0,1:T(2,128)S(1)}, s32[32,2]{0,1:T(2,128)}, u32[]{:S(2)}) %copy-start) | copy-done | bytes 280
  3.3 33.5 %conditional.1 = ((f32[1,4,384]{2,1,0:T(4,128)S(1)}, f32[1,4,384]{2,1,0:T(4,128)S(1)})) conditional(s32[]{:T(128)} %clamp.3, (f32[2,12,64]{2,0,1:T(2,128)}, bf16[2,64,1536]{2,1,0:T(8,128)(2,1)}, s32[2,32]{1,0:T(2,128)S(1)}) %tuple.38, (f32[2,12,64]{2,0,1:T(2,128)}, bf16[2,64,1536]{2,1,0:T(8,128)(2,1)}, ...), branch_computations={%region_1.2_spmd, %region_2.3_spmd, %region_3.4_spmd, %region_4.5_... | conditional | flops 1207959552 | bytes 393224 | solution.py:442
  3.3 33.5 %branch_2_fun.1 = (f32[1,4,384]{2,1,0:T(4,128)S(1)}, f32[1,4,384]{2,1,0:T(4,128)S(1)}) custom-call(bf16[2,64,1536]{2,1,0:T(8,128)(2,1)} %get-tuple-element.62.codes_ref, f32[12,2,64]{2,1,0:T(2,128)} %bitcast.17, s32[2,32]{1,0:T(2,128)S(1)} %get-tuple-element.32.pairs_ref), custom_call_target="tpu_custom_call" | custom-call | flops 1207959552 | bytes 393216 | tf_op jit(solution)/shard_map/cond/branch_2_fun/pallas_call | solution.py:365
  36.8 0.6 %copy.31 = f32[1,4,384]{2,1,0:T(4,128)} copy(f32[1,4,384]{2,1,0:T(4,128)S(1)} %get-tuple-element.74) | data formatting | bytes 12288
  37.4 0.6 %copy.32 = f32[1,4,384]{2,1,0:T(4,128)} copy(f32[1,4,384]{2,1,0:T(4,128)S(1)} %get-tuple-element.75) | data formatting | bytes 12288
Async XLA Ops:
  2.6 0.7 %copy-start = (s32[32,2]{0,1:T(2,128)S(1)}, s32[32,2]{0,1:T(2,128)}, u32[]{:S(2)}) copy-start(s32[32,2]{0,1:T(2,128)} %param.9) | copy-start | bytes 772

commit v4 on v3

--- a/solution.py
+++ b/solution.py
@@ -122,7 +122,7 @@
 
 def pair_kernel(
     order, turns, n, groups,
-    codes_ref, scales_ref, pairs_ref, left_out, right_out,
+    codes_ref, scales_ref, pairs_ref, out_ref,
     codes, acts, send_left, send_right, left_rows, right_rows, turned, inv_left, best, right_row,
     left_stage, right_stage, left_got, right_got,
     load_sem, left_send_sem, left_sem, right_send_sem, right_sem, out_send_sem, left_got_sem, right_got_sem,
@@ -351,22 +351,22 @@
         share = 0
         for k in range(groups):
             share = share + jnp.where(offset == order[k], k, 0)
-        left_out[0, s : s + 1, :] = left_got[share]
-        right_out[0, s : s + 1, :] = right_got[share]
+        out_ref[s : s + 1, :] = left_got[share]
+        out_ref[groups + s : groups + s + 1, :] = right_got[share]
 
 
 def pair_call(order, turns, n, groups, collective_id, unit_codes, block_scales, pairs):
     per_device, rows, units = unit_codes.shape
     chunks = units // CHUNK
     part = units // groups
-    out = jax.ShapeDtypeStruct((1, groups, part), jnp.float32)
+    out = jax.ShapeDtypeStruct((2 * groups, part), jnp.float32)
     vmem = pl.BlockSpec(memory_space=pltpu.VMEM)
     dma = pltpu.SemaphoreType.DMA
     return pl.pallas_call(
         functools.partial(pair_kernel, order, turns, n, groups),
-        out_shape=(out, out),
+        out_shape=out,
         in_specs=[pl.BlockSpec(memory_space=pl.ANY), vmem, pl.BlockSpec(memory_space=pltpu.SMEM)],
-        out_specs=(vmem, vmem),
+        out_specs=vmem,
         scratch_shapes=[
             pltpu.VMEM((per_device, rows, units), jnp.bfloat16),
             pltpu.VMEM((per_device, chunks, rows, CHUNK), jnp.bfloat16),
@@ -439,7 +439,8 @@
     for at, members in enumerate(sets):
         order, turns = TURNS.get(members, (members, (0,) * n)) if (n, groups) == (8, 4) else (members, (0,) * n)
         calls.append(functools.partial(pair_call, order, turns, n, groups, at))
-    return lax.switch(branch, calls, unit_codes, block_scales, pair_list.T)
+    best = lax.switch(branch, calls, unit_codes, block_scales, pair_list.T)
+    return (best[None, :slots], best[None, slots:])
 
 
 def solution(mesh):

time: 37.6 us -> 36.2 us (0.963); the launches traced: 38 us -> 35.6 us
  Pallas kernels: 33.5 us -> 31.7 us
  local copies, waits for them, and re-layouts: 1.86 us -> 1.28 us
    pallas_call x1, Pallas kernels: 33.5 us -> 31.7 us  [pair_call(): pl.pallas_call(functools.partial(pair_kernel, order, turns, n, groups), o...]
    unnamed x4 -> x2, local copies, waits for them, and re-layouts: 1.86 us -> 0.67 us
    broadcast_in_dim x0 -> x1, local copies, waits for them, and re-layouts: none -> 0.6 us  [body(): return (best[None, :slots], best[None, slots:])]
where the time goes in v4:
time: 36.2 us; the launch traced here: 35.6 us
  Pallas kernels  31.7 us (88%)
  other arithmetic  1.33 us (4%)
  between operations  1.3 us (4%)
  local copies, waits for them, and re-layouts  1.28 us (4%)
    pallas_call x1, Pallas kernels, pair_call(): pl.pallas_call(functools.partial(pair_kernel, order, turns, n, groups), o...  31.7 us
    reduce_sum x1, other arithmetic, body(): jnp.sum(sum((jnp.where(offsets == offset, at, 0) for offset, at in free)))  1.33 us

profile of v4, /device:TPU:0, one launch (start us, length us, event | category | flops | bytes accessed | tf_op | source)
XLA Modules:
  0.0 35.6 jit_solution(4729490511183194387)
XLA Ops:
  0.6 1.3 %fusion.2 = s32[]{:T(128)} fusion(s32[32,2]{0,1:T(2,128)} %param.9), kind=kLoop, calls=%fused_computation.11 | loop fusion | flops 95 | bytes 20 | tf_op jit(solution)/shard_map/reduce_sum | solution.py:432
  2.6 0.0 copy-start
  2.6 0.7 %copy-done = s32[32,2]{0,1:T(2,128)S(1)} copy-done((s32[32,2]{0,1:T(2,128)S(1)}, s32[32,2]{0,1:T(2,128)}, u32[]{:S(2)}) %copy-start) | copy-done | bytes 280
  3.3 31.7 %conditional.1 = (f32[8,384]{1,0:T(8,128)S(1)}) conditional(s32[]{:T(128)} %clamp.3, (f32[2,12,64]{2,0,1:T(2,128)}, bf16[2,64,1536]{2,1,0:T(8,128)(2,1)}, s32[2,32]{1,0:T(2,128)S(1)}) %tuple.27, (f32[2,12,64]{2,0,1:T(2,128)}, bf16[2,64,1536]{2,1,0:T(8,128)(2,1)}, s32[2,32]{1,0:T(2,128)S(1)}) %tuple.28, ...), branch_computations={%region_1.2_spmd, %region_2.3_spmd, %region_3.4_spmd, %region_4.5_... | conditional | flops 1207959552 | bytes 393224 | solution.py:442
  3.3 31.7 %branch_3_fun.1 = f32[8,384]{1,0:T(8,128)S(1)} custom-call(bf16[2,64,1536]{2,1,0:T(8,128)(2,1)} %get-tuple-element.58.codes_ref, f32[12,2,64]{2,1,0:T(2,128)} %bitcast.22, s32[2,32]{1,0:T(2,128)S(1)} %get-tuple-element.40.pairs_ref), custom_call_target="tpu_custom_call" | custom-call | flops 1207959552 | bytes 393216 | tf_op jit(solution)/shard_map/cond/branch_3_fun/pallas_call | solution.py:365
  35.0 0.6 %slice_bitcast_fusion = (f32[1,4,384]{2,1,0:T(4,128)}, f32[1,4,384]{2,1,0:T(4,128)}) fusion(f32[8,384]{1,0:T(8,128)S(1)} %get-tuple-element.61), kind=kLoop, calls=%fused_computation | loop fusion | bytes 24576 | tf_op jit(solution)/shard_map/broadcast_in_dim | solution.py:443
Async XLA Ops:
  2.6 0.7 %copy-start = (s32[32,2]{0,1:T(2,128)S(1)}, s32[32,2]{0,1:T(2,128)}, u32[]{:S(2)}) copy-start(s32[32,2]{0,1:T(2,128)} %param.9) | copy-start | bytes 772

commit v5 on v4

--- a/solution.py
+++ b/solution.py
@@ -426,10 +426,16 @@
     )
     if not sets or not fits:
         return general_body(unit_codes, block_scales, pair_list)
+    columns = pair_list.T
     offsets = pair_list[:slots, 1] // per_device
     if slots == 4 and n > 4:
         free = [(sum(members) - 1 - n // 2 - (n - 1), at) for at, members in enumerate(sets)]
+        side = lax.broadcasted_iota(jnp.int32, columns.shape, 0)
+        slot = lax.broadcasted_iota(jnp.int32, columns.shape, 1)
+        offsets = jnp.where((side == 1) & (slot < slots), columns // per_device, 0)
         branch = jnp.sum(sum(jnp.where(offsets == offset, at, 0) for offset, at in free))
+        columns = jnp.where(side == 0, columns % per_device, columns)
+        branch, columns = lax.optimization_barrier((branch, columns))
     else:
         branch = 0
         for at, members in enumerate(sets):
@@ -439,7 +445,7 @@
     for at, members in enumerate(sets):
         order, turns = TURNS.get(members, (members, (0,) * n)) if (n, groups) == (8, 4) else (members, (0,) * n)
         calls.append(functools.partial(pair_call, order, turns, n, groups, at))
-    best = lax.switch(branch, calls, unit_codes, block_scales, pair_list.T)
+    best = lax.switch(branch, calls, unit_codes, block_scales, columns)
     return (best[None, :slots], best[None, slots:])
 
 

time: 36.2 us -> 35.8 us (0.989)
  other arithmetic: 1.33 us -> 0.72 us
  Pallas kernels: 31.7 us -> 32.2 us
    reduce_sum x1 -> x0, other arithmetic: 1.33 us -> none  [body(): jnp.sum(sum((jnp.where(offsets == offset, at, 0) for offset, at in free)))]
    select_n x0 -> x1, other arithmetic: none -> 0.7 us  [body(): columns = jnp.where(side == 0, columns % per_device, columns)]
    pallas_call x1, Pallas kernels: 31.7 us -> 32.2 us  [pair_call(): pl.pallas_call(functools.partial(pair_kernel, order, turns, n, groups), o...]
where the time goes in v5:
time: 35.8 us; the launch traced here: 35.5 us
  Pallas kernels  32.2 us (90%)
  between operations  1.31 us (4%)
  local copies, waits for them, and re-layouts  1.28 us (4%)
  other arithmetic  0.72 us (2%)
    pallas_call x1, Pallas kernels, pair_call(): pl.pallas_call(functools.partial(pair_kernel, order, turns, n, groups), o...  32.2 us

profile of v5, /device:TPU:0, one launch (start us, length us, event | category | flops | bytes accessed | tf_op | source)
XLA Modules:
  0.0 35.5 jit_solution(13310766042104135958)
XLA Ops:
  0.7 0.0 copy-start
  0.7 0.7 %copy-done = s32[32,2]{0,1:T(2,128)S(1)} copy-done((s32[32,2]{0,1:T(2,128)S(1)}, s32[32,2]{0,1:T(2,128)}, u32[]{:S(2)}) %copy-start) | copy-done | bytes 280
  1.3 0.7 %fusion.2 = (s32[2,32]{1,0:T(2,128)S(1)}, s32[]{:T(128)}) fusion(s32[32,2]{0,1:T(2,128)S(1)} %copy-done, pred[2]{0:T(512)(128)(4,1)S(1)} %get-tuple-element.51, pred[32]{0:T(512)(128)(4,1)S(1)} %iota_compare_fusion.1, pred[2]{0:T(512)(128)(4,1)S(1)} %get-tuple-element.52), kind=kLoop, calls=%fused_computation.13 | loop fusion | flops 1983 | bytes 552 | tf_op jit(solution)/shard_map/jit(_where)/select_n | solution.py:437
  2.7 32.2 %conditional.1 = (f32[8,384]{1,0:T(8,128)S(1)}) conditional(s32[]{:T(128)} %clamp.3, (f32[2,12,64]{2,0,1:T(2,128)}, bf16[2,64,1536]{2,1,0:T(8,128)(2,1)}, s32[2,32]{1,0:T(2,128)S(1)}) %tuple.22, (f32[2,12,64]{2,0,1:T(2,128)}, bf16[2,64,1536]{2,1,0:T(8,128)(2,1)}, s32[2,32]{1,0:T(2,128)S(1)}) %tuple.22, ...), branch_computations={%region_1.2_spmd, %region_2.3_spmd, %region_3.4_spmd, %region_4.5_... | conditional | flops 1207959552 | bytes 393224 | solution.py:448
  2.7 32.2 %branch_1_fun.1 = f32[8,384]{1,0:T(8,128)S(1)} custom-call(bf16[2,64,1536]{2,1,0:T(8,128)(2,1)} %get-tuple-element.32.codes_ref, f32[12,2,64]{2,1,0:T(2,128)} %bitcast.32, s32[2,32]{1,0:T(2,128)S(1)} %get-tuple-element.34.pairs_ref), custom_call_target="tpu_custom_call" | custom-call | flops 1207959552 | bytes 393216 | tf_op jit(solution)/shard_map/cond/branch_1_fun/pallas_call | solution.py:365
  34.9 0.6 %slice_bitcast_fusion = (f32[1,4,384]{2,1,0:T(4,128)}, f32[1,4,384]{2,1,0:T(4,128)}) fusion(f32[8,384]{1,0:T(8,128)S(1)} %get-tuple-element.53), kind=kLoop, calls=%fused_computation | loop fusion | bytes 24576 | tf_op jit(solution)/shard_map/broadcast_in_dim | solution.py:449
  (2 shorter events, 0.0 us)
Async XLA Ops:
  0.7 0.7 %copy-start = (s32[32,2]{0,1:T(2,128)S(1)}, s32[32,2]{0,1:T(2,128)}, u32[]{:S(2)}) copy-start(s32[32,2]{0,1:T(2,128)} %param.9) | copy-start | bytes 772

commit v6 on v5

--- a/solution.py
+++ b/solution.py
@@ -122,15 +122,15 @@
 
 def pair_kernel(
     order, turns, n, groups,
-    codes_ref, scales_ref, pairs_ref, out_ref,
-    codes, acts, send_left, send_right, left_rows, right_rows, turned, inv_left, best, right_row,
+    codes_ref, scales_hbm, pairs_hbm, out_ref,
+    scales_ref, pairs_ref, codes, acts, send_left, send_right, left_rows, right_rows, turned, inv_left, best, right_row,
     left_stage, right_stage, left_got, right_got,
-    load_sem, left_send_sem, left_sem, right_send_sem, right_sem, out_send_sem, left_got_sem, right_got_sem,
+    load_sem, scales_sem, pairs_sem, left_send_sem, left_sem, right_send_sem, right_sem, out_send_sem, left_got_sem, right_got_sem,
 ):
     me = lax.axis_index("expert")
     dp = lax.axis_index("dp")
     per_device, rows, units = codes_ref.shape
-    blocks = scales_ref.shape[0]
+    blocks = scales_hbm.shape[0]
     width = units // blocks
     chunks = units // CHUNK
     part = units // groups
@@ -157,7 +157,12 @@
         pl.semaphore_signal(barrier, inc=1, device_id=device, device_id_type=MESH)
 
     load = pltpu.make_async_copy(codes_ref, codes, load_sem)
+    load_scales = pltpu.make_async_copy(scales_hbm, scales_ref, scales_sem)
+    load_pairs = pltpu.make_async_copy(pairs_hbm, pairs_ref, pairs_sem)
+    load_pairs.start()
+    load_scales.start()
     load.start()
+    load_pairs.wait()
 
     def slot_of(offset):
         slot = 0
@@ -173,6 +178,7 @@
     left_pick = [
         chosen(me, slot_of(pick(share_of(member, me), order)), 0) for member in others + [dp]
     ]
+    load_scales.wait()
     factors = [scales_ref[:, expert, :].T for expert in range(per_device)]
 
     def scale_and_stage(c):
@@ -360,14 +366,16 @@
     chunks = units // CHUNK
     part = units // groups
     out = jax.ShapeDtypeStruct((2 * groups, part), jnp.float32)
-    vmem = pl.BlockSpec(memory_space=pltpu.VMEM)
+    anywhere = pl.BlockSpec(memory_space=pl.ANY)
     dma = pltpu.SemaphoreType.DMA
     return pl.pallas_call(
         functools.partial(pair_kernel, order, turns, n, groups),
         out_shape=out,
-        in_specs=[pl.BlockSpec(memory_space=pl.ANY), vmem, pl.BlockSpec(memory_space=pltpu.SMEM)],
-        out_specs=vmem,
+        in_specs=[anywhere, anywhere, anywhere],
+        out_specs=pl.BlockSpec(memory_space=pltpu.VMEM),
         scratch_shapes=[
+            pltpu.VMEM((block_scales.shape[1], per_device, rows), jnp.float32),
+            pltpu.SMEM(pairs.shape, jnp.int32),
             pltpu.VMEM((per_device, rows, units), jnp.bfloat16),
             pltpu.VMEM((per_device, chunks, rows, CHUNK), jnp.bfloat16),
             pltpu.VMEM((groups - 1, chunks, rows, CHUNK), jnp.bfloat16),
@@ -382,6 +390,8 @@
             pltpu.VMEM((groups, 1, part), jnp.float32),
             pltpu.VMEM((groups, 1, part), jnp.float32),
             pltpu.VMEM((groups, 1, part), jnp.float32),
+            dma,
+            dma,
             dma,
             dma((groups - 1, chunks)),
             dma((chunks, groups)),

time: 35.8 us -> 35 us (0.978); the launches traced: 35.5 us -> 34.4 us
  Pallas kernels: 32.2 us -> 31 us
    pallas_call x1, Pallas kernels: 32.2 us -> 31 us  [pair_call(): pl.pallas_call(functools.partial(pair_kernel, order, turns, n, groups), o...]
where the time goes in v6:
time: 35 us; the launch traced here: 34.4 us
  Pallas kernels  31 us (89%)
  between operations  1.31 us (4%)
  local copies, waits for them, and re-layouts  1.28 us (4%)
  other arithmetic  0.72 us (2%)
    pallas_call x1, Pallas kernels, pair_call(): pl.pallas_call(functools.partial(pair_kernel, order, turns, n, groups), o...  31 us
    select_n x1, other arithmetic, body(): columns = jnp.where(side == 0, columns % per_device, columns)  0.7 us

profile of v6, /device:TPU:0, one launch (start us, length us, event | category | flops | bytes accessed | tf_op | source)
XLA Modules:
  0.0 34.4 jit_solution(18213389496387428090)
XLA Ops:
  0.7 0.0 copy-start
  0.7 0.7 %copy-done = s32[32,2]{0,1:T(2,128)S(1)} copy-done((s32[32,2]{0,1:T(2,128)S(1)}, s32[32,2]{0,1:T(2,128)}, u32[]{:S(2)}) %copy-start) | copy-done | bytes 280
  1.3 0.7 %fusion.2 = (s32[2,32]{1,0:T(2,128)S(1)}, s32[]{:T(128)}) fusion(s32[32,2]{0,1:T(2,128)S(1)} %copy-done, pred[2]{0:T(512)(128)(4,1)S(1)} %get-tuple-element.51, pred[32]{0:T(512)(128)(4,1)S(1)} %iota_compare_fusion.1, pred[2]{0:T(512)(128)(4,1)S(1)} %get-tuple-element.52), kind=kLoop, calls=%fused_computation.13 | loop fusion | flops 1983 | bytes 552 | tf_op jit(solution)/shard_map/jit(_where)/select_n | solution.py:447
  2.7 31.0 %conditional.1 = (f32[8,384]{1,0:T(8,128)S(1)}) conditional(s32[]{:T(128)} %clamp.3, (f32[2,12,64]{2,0,1:T(2,128)}, bf16[2,64,1536]{2,1,0:T(8,128)(2,1)}, s32[2,32]{1,0:T(2,128)S(1)}) %tuple.22, (f32[2,12,64]{2,0,1:T(2,128)}, bf16[2,64,1536]{2,1,0:T(8,128)(2,1)}, s32[2,32]{1,0:T(2,128)S(1)}) %tuple.22, ...), branch_computations={%region_1.2_spmd, %region_2.3_spmd, %region_3.4_spmd, %region_4.5_... | conditional | flops 1207959552 | bytes 393224 | solution.py:458
  2.7 31.0 %branch_3_fun.1 = f32[8,384]{1,0:T(8,128)S(1)} custom-call(bf16[2,64,1536]{2,1,0:T(8,128)(2,1)} %get-tuple-element.38.codes_ref, f32[12,2,64]{2,1,0:T(2,128)} %bitcast.34, s32[2,32]{1,0:T(2,128)S(1)} %get-tuple-element.40.pairs_hbm), custom_call_target="tpu_custom_call" | custom-call | flops 1207959552 | bytes 393216 | tf_op jit(solution)/shard_map/cond/branch_3_fun/pallas_call | solution.py:371
  33.7 0.6 %slice_bitcast_fusion = (f32[1,4,384]{2,1,0:T(4,128)}, f32[1,4,384]{2,1,0:T(4,128)}) fusion(f32[8,384]{1,0:T(8,128)S(1)} %get-tuple-element.53), kind=kLoop, calls=%fused_computation | loop fusion | bytes 24576 | tf_op jit(solution)/shard_map/broadcast_in_dim | solution.py:459
  (2 shorter events, 0.0 us)
Async XLA Ops:
  0.7 0.7 %copy-start = (s32[32,2]{0,1:T(2,128)S(1)}, s32[32,2]{0,1:T(2,128)}, u32[]{:S(2)}) copy-start(s32[32,2]{0,1:T(2,128)} %param.9) | copy-start | bytes 772

commit v7 on v6

--- a/solution.py
+++ b/solution.py
@@ -217,6 +217,7 @@
 
     load.wait()
     ahead = (2 * chunks + 2) // 3
+    far_first = sorted(range(groups), key=lambda k: -min(order[k], n - order[k]))
     staged = 0
     for c in range(chunks):
         lefts = range(c * chunks // ahead, (c + 1) * chunks // ahead) if c < ahead else range(0)
@@ -225,7 +226,7 @@
             staged += 1
         if c == 0:
             pl.semaphore_wait(barrier, len(greeted))
-        for k in range(groups):
+        for k in far_first:
             right_copy(k, c).start()
         for at in lefts:
             for r in range(groups - 1):
@@ -251,8 +252,18 @@
         inv_left[at, :] = jnp.broadcast_to(inverse, (128, CHUNK)).T
         turned[at, :] = block.T
 
+    def sent(c):
+        for r in range(groups - 1):
+            left_copy(r, c).wait_send()
+        for k in range(groups):
+            right_copy(k, c).wait_send()
+
     @pl.loop(0, chunks)
     def _(c):
+        @pl.when(c >= 2)
+        def _():
+            sent(c - 2)
+
         for member in range(groups):
             pltpu.make_async_remote_copy(
                 src_ref=send_right.at[0, 0],
@@ -321,12 +332,16 @@
         left_result(r).start()
     left_got[mine] = left_stage[dp]
 
-    @pl.loop(0, chunks)
-    def _(c):
-        for r in range(groups - 1):
-            left_copy(r, c).wait_send()
+    share_at = []
+    for s in range(groups):
+        offset = pairs_ref[1, s] // per_device
+        share = 0
         for k in range(groups):
-            right_copy(k, c).wait_send()
+            share = share + jnp.where(offset == order[k], k, 0)
+        share_at.append(share)
+
+    for c in range(max(chunks - 2, 0), chunks):
+        sent(c)
 
     for other in others:
         share = share_of(other, me)
@@ -353,12 +368,8 @@
         left_result(r).wait_send()
 
     for s in range(groups):
-        offset = pairs_ref[1, s] // per_device
-        share = 0
-        for k in range(groups):
-            share = share + jnp.where(offset == order[k], k, 0)
-        out_ref[s : s + 1, :] = left_got[share]
-        out_ref[groups + s : groups + s + 1, :] = right_got[share]
+        out_ref[s : s + 1, :] = left_got[share_at[s]]
+        out_ref[groups + s : groups + s + 1, :] = right_got[share_at[s]]
 
 
 def pair_call(order, turns, n, groups, collective_id, unit_codes, block_scales, pairs):

time: 35 us -> 34.9 us (level)
  no operation moved by 1% of the time
where the time goes in v7:
time: 34.9 us; the launch traced here: 34.4 us
  Pallas kernels  31 us (89%)
  between operations  1.31 us (4%)
  local copies, waits for them, and re-layouts  1.28 us (4%)
  other arithmetic  0.72 us (2%)
    pallas_call x1, Pallas kernels, pair_call(): pl.pallas_call(functools.partial(pair_kernel, order, turns, n, groups), o...  31 us
    select_n x1, other arithmetic, body(): columns = jnp.where(side == 0, columns % per_device, columns)  0.7 us

profile of v7, /device:TPU:0, one launch (start us, length us, event | category | flops | bytes accessed | tf_op | source)
XLA Modules:
  0.0 34.4 jit_solution(9989544072154108014)
XLA Ops:
  0.7 0.0 copy-start
  0.7 0.7 %copy-done = s32[32,2]{0,1:T(2,128)S(1)} copy-done((s32[32,2]{0,1:T(2,128)S(1)}, s32[32,2]{0,1:T(2,128)}, u32[]{:S(2)}) %copy-start) | copy-done | bytes 280
  1.3 0.7 %fusion.2 = (s32[2,32]{1,0:T(2,128)S(1)}, s32[]{:T(128)}) fusion(s32[32,2]{0,1:T(2,128)S(1)} %copy-done, pred[2]{0:T(512)(128)(4,1)S(1)} %get-tuple-element.51, pred[32]{0:T(512)(128)(4,1)S(1)} %iota_compare_fusion.1, pred[2]{0:T(512)(128)(4,1)S(1)} %get-tuple-element.52), kind=kLoop, calls=%fused_computation.13 | loop fusion | flops 1983 | bytes 552 | tf_op jit(solution)/shard_map/jit(_where)/select_n | solution.py:458
  2.7 31.1 %conditional.1 = (f32[8,384]{1,0:T(8,128)S(1)}) conditional(s32[]{:T(128)} %clamp.3, (f32[2,12,64]{2,0,1:T(2,128)}, bf16[2,64,1536]{2,1,0:T(8,128)(2,1)}, s32[2,32]{1,0:T(2,128)S(1)}) %tuple.22, (f32[2,12,64]{2,0,1:T(2,128)}, bf16[2,64,1536]{2,1,0:T(8,128)(2,1)}, s32[2,32]{1,0:T(2,128)S(1)}) %tuple.22, ...), branch_computations={%region_1.2_spmd, %region_2.3_spmd, %region_3.4_spmd, %region_4.5_... | conditional | flops 1207959552 | bytes 393224 | solution.py:469
  2.7 31.0 %branch_3_fun.1 = f32[8,384]{1,0:T(8,128)S(1)} custom-call(bf16[2,64,1536]{2,1,0:T(8,128)(2,1)} %get-tuple-element.38.codes_ref, f32[12,2,64]{2,1,0:T(2,128)} %bitcast.34, s32[2,32]{1,0:T(2,128)S(1)} %get-tuple-element.40.pairs_hbm), custom_call_target="tpu_custom_call" | custom-call | flops 1207959552 | bytes 393216 | tf_op jit(solution)/shard_map/cond/branch_3_fun/pallas_call | solution.py:382
  33.8 0.6 %slice_bitcast_fusion = (f32[1,4,384]{2,1,0:T(4,128)}, f32[1,4,384]{2,1,0:T(4,128)}) fusion(f32[8,384]{1,0:T(8,128)S(1)} %get-tuple-element.53), kind=kLoop, calls=%fused_computation | loop fusion | bytes 24576 | tf_op jit(solution)/shard_map/broadcast_in_dim | solution.py:470
  (2 shorter events, 0.0 us)
Async XLA Ops:
  0.7 0.7 %copy-start = (s32[32,2]{0,1:T(2,128)S(1)}, s32[32,2]{0,1:T(2,128)}, u32[]{:S(2)}) copy-start(s32[32,2]{0,1:T(2,128)} %param.9) | copy-start | bytes 772

commit v8 on v7

--- a/solution.py
+++ b/solution.py
@@ -148,13 +148,7 @@
     askers = [(me - order[k] + n) % n for k in range(groups)]
     ask_member = [member_of(k, askers[k]) for k in range(groups)]
     others = [(dp + r) % groups for r in range(1, groups)]
-
-    barrier = pltpu.get_barrier_semaphore()
-    greeted = [(other, me) for other in others]
-    greeted += [(ask_member[k], askers[k]) for k in range(groups)]
-    greeted += [(member, partner) for member in range(groups)]
-    for device in greeted:
-        pl.semaphore_signal(barrier, inc=1, device_id=device, device_id_type=MESH)
+    far_first = sorted(range(groups), key=lambda k: -min(order[k], n - order[k]))
 
     load = pltpu.make_async_copy(codes_ref, codes, load_sem)
     load_scales = pltpu.make_async_copy(scales_hbm, scales_ref, scales_sem)
@@ -162,6 +156,14 @@
     load_pairs.start()
     load_scales.start()
     load.start()
+
+    barrier = pltpu.get_barrier_semaphore()
+    greeted = [(ask_member[k], askers[k]) for k in far_first]
+    greeted += [(member, partner) for member in range(groups)]
+    greeted += [(other, me) for other in others]
+    for device in greeted:
+        pl.semaphore_signal(barrier, inc=1, device_id=device, device_id_type=MESH)
+
     load_pairs.wait()
 
     def slot_of(offset):
@@ -217,7 +219,6 @@
 
     load.wait()
     ahead = (2 * chunks + 2) // 3
-    far_first = sorted(range(groups), key=lambda k: -min(order[k], n - order[k]))
     staged = 0
     for c in range(chunks):
         lefts = range(c * chunks // ahead, (c + 1) * chunks // ahead) if c < ahead else range(0)

time: 34.9 us -> 36.3 us (1.040)
  Pallas kernels: 31 us -> 32.7 us
    pallas_call x1, Pallas kernels: 31 us -> 32.7 us  [pair_call(): pl.pallas_call(functools.partial(pair_kernel, order, turns, n, groups), o...]
where the time goes in v8:
time: 36.3 us; the launch traced here: 36.1 us
  Pallas kernels  32.7 us (90%)
  between operations  1.31 us (4%)
  local copies, waits for them, and re-layouts  1.28 us (4%)
  other arithmetic  0.72 us (2%)
    pallas_call x1, Pallas kernels, pair_call(): pl.pallas_call(functools.partial(pair_kernel, order, turns, n, groups), o...  32.7 us

profile of v8, /device:TPU:0, one launch (start us, length us, event | category | flops | bytes accessed | tf_op | source)
XLA Modules:
  0.0 36.1 jit_solution(2938966423993811337)
XLA Ops:
  0.7 0.0 copy-start
  0.7 0.7 %copy-done = s32[32,2]{0,1:T(2,128)S(1)} copy-done((s32[32,2]{0,1:T(2,128)S(1)}, s32[32,2]{0,1:T(2,128)}, u32[]{:S(2)}) %copy-start) | copy-done | bytes 280
  1.3 0.7 %fusion.2 = (s32[2,32]{1,0:T(2,128)S(1)}, s32[]{:T(128)}) fusion(s32[32,2]{0,1:T(2,128)S(1)} %copy-done, pred[2]{0:T(512)(128)(4,1)S(1)} %get-tuple-element.51, pred[32]{0:T(512)(128)(4,1)S(1)} %iota_compare_fusion.1, pred[2]{0:T(512)(128)(4,1)S(1)} %get-tuple-element.52), kind=kLoop, calls=%fused_computation.13 | loop fusion | flops 1983 | bytes 552 | tf_op jit(solution)/shard_map/jit(_where)/select_n | solution.py:459
  2.7 32.8 %conditional.1 = (f32[8,384]{1,0:T(8,128)S(1)}) conditional(s32[]{:T(128)} %clamp.3, (f32[2,12,64]{2,0,1:T(2,128)}, bf16[2,64,1536]{2,1,0:T(8,128)(2,1)}, s32[2,32]{1,0:T(2,128)S(1)}) %tuple.22, (f32[2,12,64]{2,0,1:T(2,128)}, bf16[2,64,1536]{2,1,0:T(8,128)(2,1)}, s32[2,32]{1,0:T(2,128)S(1)}) %tuple.22, ...), branch_computations={%region_1.2_spmd, %region_2.3_spmd, %region_3.4_spmd, %region_4.5_... | conditional | flops 1207959552 | bytes 393224 | solution.py:470
  2.7 32.7 %branch_0_fun.1 = f32[8,384]{1,0:T(8,128)S(1)} custom-call(bf16[2,64,1536]{2,1,0:T(8,128)(2,1)} %get-tuple-element.25.codes_ref, f32[12,2,64]{2,1,0:T(2,128)} %bitcast.31, s32[2,32]{1,0:T(2,128)S(1)} %get-tuple-element.27.pairs_hbm), custom_call_target="tpu_custom_call" | custom-call | flops 1207959552 | bytes 393216 | tf_op jit(solution)/shard_map/cond/branch_0_fun/pallas_call | solution.py:383
  35.5 0.6 %slice_bitcast_fusion = (f32[1,4,384]{2,1,0:T(4,128)}, f32[1,4,384]{2,1,0:T(4,128)}) fusion(f32[8,384]{1,0:T(8,128)S(1)} %get-tuple-element.53), kind=kLoop, calls=%fused_computation | loop fusion | bytes 24576 | tf_op jit(solution)/shard_map/broadcast_in_dim | solution.py:471
  (2 shorter events, 0.0 us)
Async XLA Ops:
  0.7 0.7 %copy-start = (s32[32,2]{0,1:T(2,128)S(1)}, s32[32,2]{0,1:T(2,128)}, u32[]{:S(2)}) copy-start(s32[32,2]{0,1:T(2,128)} %param.9) | copy-start | bytes 772

commit v9 on v8

--- a/solution.py
+++ b/solution.py
@@ -103,7 +103,7 @@
 CHUNK = 256
 MAX_BRANCHES = 8
 TURNS = {
-    (1, 2, 4, 7): ((1, 7, 4, 2), (1, 1, 2, 2, 0, 3, 1, 0)),
+    (1, 2, 4, 7): ((7, 1, 2, 4), (0, 3, 3, 2, 3, 1, 2, 0)),
     (1, 3, 4, 7): ((1, 4, 7, 3), (0, 1, 3, 0, 3, 1, 2, 0)),
     (1, 4, 5, 7): ((1, 4, 7, 5), (0, 0, 1, 3, 3, 2, 1, 2)),
     (1, 4, 6, 7): ((1, 7, 6, 4), (0, 2, 1, 3, 2, 3, 3, 0)),

time: 36.3 us -> 34.9 us (0.961)
  Pallas kernels: 32.7 us -> 31 us
    pallas_call x1, Pallas kernels: 32.7 us -> 31 us  [pair_call(): pl.pallas_call(functools.partial(pair_kernel, order, turns, n, groups), o...]
where the time goes in v9:
time: 34.9 us; the launch traced here: 34.4 us
  Pallas kernels  31 us (89%)
  between operations  1.31 us (4%)
  local copies, waits for them, and re-layouts  1.28 us (4%)
  other arithmetic  0.72 us (2%)
    pallas_call x1, Pallas kernels, pair_call(): pl.pallas_call(functools.partial(pair_kernel, order, turns, n, groups), o...  31 us
    select_n x1, other arithmetic, body(): columns = jnp.where(side == 0, columns % per_device, columns)  0.7 us

profile of v9, /device:TPU:0, one launch (start us, length us, event | category | flops | bytes accessed | tf_op | source)
XLA Modules:
  0.0 34.4 jit_solution(11421354737953775437)
XLA Ops:
  0.7 0.0 copy-start
  0.7 0.7 %copy-done = s32[32,2]{0,1:T(2,128)S(1)} copy-done((s32[32,2]{0,1:T(2,128)S(1)}, s32[32,2]{0,1:T(2,128)}, u32[]{:S(2)}) %copy-start) | copy-done | bytes 280
  1.3 0.7 %fusion.2 = (s32[2,32]{1,0:T(2,128)S(1)}, s32[]{:T(128)}) fusion(s32[32,2]{0,1:T(2,128)S(1)} %copy-done, pred[2]{0:T(512)(128)(4,1)S(1)} %get-tuple-element.51, pred[32]{0:T(512)(128)(4,1)S(1)} %iota_compare_fusion.1, pred[2]{0:T(512)(128)(4,1)S(1)} %get-tuple-element.52), kind=kLoop, calls=%fused_computation.13 | loop fusion | flops 1983 | bytes 552 | tf_op jit(solution)/shard_map/jit(_where)/select_n | solution.py:459
  2.7 31.1 %conditional.1 = (f32[8,384]{1,0:T(8,128)S(1)}) conditional(s32[]{:T(128)} %clamp.3, (f32[2,12,64]{2,0,1:T(2,128)}, bf16[2,64,1536]{2,1,0:T(8,128)(2,1)}, s32[2,32]{1,0:T(2,128)S(1)}) %tuple.22, (f32[2,12,64]{2,0,1:T(2,128)}, bf16[2,64,1536]{2,1,0:T(8,128)(2,1)}, s32[2,32]{1,0:T(2,128)S(1)}) %tuple.22, ...), branch_computations={%region_1.2_spmd, %region_2.3_spmd, %region_3.4_spmd, %region_4.5_... | conditional | flops 1207959552 | bytes 393224 | solution.py:470
  2.7 31.0 %branch_3_fun.1 = f32[8,384]{1,0:T(8,128)S(1)} custom-call(bf16[2,64,1536]{2,1,0:T(8,128)(2,1)} %get-tuple-element.38.codes_ref, f32[12,2,64]{2,1,0:T(2,128)} %bitcast.34, s32[2,32]{1,0:T(2,128)S(1)} %get-tuple-element.40.pairs_hbm), custom_call_target="tpu_custom_call" | custom-call | flops 1207959552 | bytes 393216 | tf_op jit(solution)/shard_map/cond/branch_3_fun/pallas_call | solution.py:383
  33.8 0.6 %slice_bitcast_fusion = (f32[1,4,384]{2,1,0:T(4,128)}, f32[1,4,384]{2,1,0:T(4,128)}) fusion(f32[8,384]{1,0:T(8,128)S(1)} %get-tuple-element.53), kind=kLoop, calls=%fused_computation | loop fusion | bytes 24576 | tf_op jit(solution)/shard_map/broadcast_in_dim | solution.py:471
  (2 shorter events, 0.0 us)
Async XLA Ops:
  0.7 0.7 %copy-start = (s32[32,2]{0,1:T(2,128)S(1)}, s32[32,2]{0,1:T(2,128)}, u32[]{:S(2)}) copy-start(s32[32,2]{0,1:T(2,128)} %param.9) | copy-start | bytes 772
